TPU v7x, 32 devices: a whole 2x2x4 slice. The times are simulated.
32 devices in a mesh: group: 2 (over y), expert: 8 (over z, x), tensor: 2 (over core).
Axes of the slice: x: 2, y: 2, z: 4, core: 2. Of those that a mesh axis runs over, the one named last changes fastest.
Arguments:
- tokens: bfloat16 [256, 6144], P(('group', 'expert', 'tensor')), parts along dimension 0, may hold values from -6 to 6
- routes: int32 [256, 4], P(('group', 'expert', 'tensor')), parts along dimension 0, may hold values from 0 to 7, all different within a row; in each aligned block of 8 rows (0 to 7, 8 to 15, ...) at most 8 rows name the same one
- gate_fixed: int32 [256, 4], P(('group', 'expert', 'tensor')), parts along dimension 0, may hold values from 1 to 65535
- w_gate: bfloat16 [8, 6144, 5376], P('expert', None, 'tensor'), may hold values from -0.078125 to 0.078125
- w_up: bfloat16 [8, 6144, 5376], P('expert', None, 'tensor'), may hold values from -0.078125 to 0.078125
- w_down: bfloat16 [8, 5376, 6144], P('expert', 'tensor'), may hold values from -0.078125 to 0.078125
Outputs:
- mixed: bfloat16 [256, 6144], P(('group', 'expert', 'tensor')), parts along dimension 0
There are 2 independent parts, one for each index of `group`. A program takes and returns all parts, laid end to end along the dimension named above; an argument that names none is the same for every part. Nothing has to cross between parts.
Inputs may be any that keep to these rules, and one draw needn't show every extreme that they name: `routes`: each row names 4 different experts. Among the 8 rows of one device no expert is named more than 8 times, and in some device an expert is named exactly 8 times.
All inputs are finite; a program needn't handle non-finite values.
Results may differ from a plain program's by a relative error of at most 0.0065.
Values may be sent and summed in bfloat16 or wider, within the bound.
A program may use at most 192 MiB of HBM per device.

v0:
```python
import jax
import jax.numpy as jnp
from jax import lax
from jax.sharding import PartitionSpec as P

CAP = 8


def slot_table(route_block, n_experts):
    flat_ids = route_block.reshape(-1)
    onehot = (flat_ids[:, None] == jnp.arange(n_experts, dtype=jnp.int32)[None, :]).astype(
        jnp.int32
    )
    earlier = jnp.cumsum(onehot, axis=0) - onehot
    slot_pos = jnp.sum(earlier * onehot, axis=1)
    target = flat_ids * CAP + slot_pos
    owner_row = jnp.arange(flat_ids.shape[0], dtype=jnp.int32) // route_block.shape[1]
    source = jnp.full((n_experts * CAP,), -1, jnp.int32).at[target].set(owner_row)
    return (source, target)


def pick_rows(table, source):
    picked = jnp.take(table, jnp.maximum(source, 0), axis=0)
    return jnp.where((source >= 0)[..., None], picked, jnp.zeros_like(picked))


def shards(tokens, routes, gate_fixed, w_gate, w_up, w_down):
    n_experts = lax.axis_size("expert")
    model_width = tokens.shape[1]
    gate_mat = w_gate[0]
    up_mat = w_up[0]
    down_mat = w_down[0]
    source, target = slot_table(routes, n_experts)
    outgoing = pick_rows(tokens, source.reshape(n_experts, CAP))
    arrived = lax.all_to_all(outgoing, "expert", split_axis=0, concat_axis=0, tiled=True)
    row_piece = lax.all_gather(arrived.reshape(-1, model_width), "tensor", axis=0, tiled=True)
    gate_val = jnp.dot(row_piece, gate_mat, preferred_element_type=jnp.float32)
    up_val = jnp.dot(row_piece, up_mat, preferred_element_type=jnp.float32)
    hidden = (jax.nn.silu(gate_val) * up_val).astype(jnp.bfloat16)
    shared_sum = lax.psum_scatter(
        jnp.dot(hidden, down_mat, preferred_element_type=jnp.float32).astype(jnp.bfloat16),
        "tensor",
        scatter_dimension=0,
        tiled=True,
    )
    expert_rows = shared_sum.reshape(n_experts, CAP, model_width)
    returned = lax.all_to_all(expert_rows, "expert", split_axis=0, concat_axis=0, tiled=True)
    chosen = jnp.take(returned.reshape(-1, model_width), target, axis=0)
    chosen = chosen.reshape(tokens.shape[0], routes.shape[1], model_width)
    fixed_val = gate_fixed.astype(jnp.float32)
    mix_weights = fixed_val / jnp.sum(fixed_val, axis=1, keepdims=True)
    mixed = jnp.sum(chosen.astype(jnp.float32) * mix_weights[:, :, None], axis=1)
    return mixed.astype(jnp.bfloat16)


def solution(mesh):
    placed = (
        P(("group", "expert", "tensor"), None),
        P(("group", "expert", "tensor"), None),
        P(("group", "expert", "tensor"), None),
        P("expert", None, "tensor"),
        P("expert", None, "tensor"),
        P("expert", "tensor", None),
    )
    return jax.shard_map(
        shards,
        mesh=mesh,
        in_specs=placed,
        out_specs=P(("group", "expert", "tensor"), None),
        check_vma=False,
    )
```

profile of v0, /device:TPU:0, one launch (start us, length us, event | category | flops | bytes accessed | tf_op | source)
XLA Modules:
  0.0 133.2 jit_solution(11240610356877962056)
XLA Ops:
  6.5 0.0 copy-start
  6.5 0.0 all-gather.2.cloned.1.call-start
  6.5 0.8 copy.10
  7.3 0.1 reshape.87
  7.4 0.1 fusion.24
  7.5 0.1 reduce_window_sum.11
  7.5 0.2 select_reduce_fusion
  7.7 0.1 mul.40
  7.8 0.7 scatter_custom_fusion
  8.5 0.1 ge.29
  8.6 0.1 le.30
  8.7 0.0 copy-done
  8.7 1.0 gather_fusion
  9.8 0.2 fusion.22
  9.9 27.3 %all_to_all.10 = bf16[8,8,6144]{2,1,0:T(8,128)(2,1)} all-to-all(bf16[8,8,6144]{2,1,0:T(8,128)(2,1)S(1)} %fusion.22), channel_id=1, replica_groups=mesh['group'=2,'expert'=8,'tensor'=2] {'expert'}, dimensions={0} | all-to-all | bytes 1572864 | tf_op jit(solution)/shard_map/all_to_all | solution.py:35
  37.2 0.0 all-gather.2.cloned.1.call-update
  37.3 0.0 reduce-scatter.2.cloned.1.call-start
  37.3 8.9 %all-gather.2.cloned.1.call-done = bf16[128,6144]{1,0:T(8,128)(2,1)} async-done(((bf16[64,6144]{1,0:T(8,128)(2,1)}), bf16[128,6144]{1,0:T(8,128)(2,1)}) %all-gather.2.cloned.1.call-update) | async-done | bytes 1572880 | tf_op jit(solution)/shard_map/all_gather | solution.py:36
  46.2 0.0 copy-start.2
  46.2 16.1 %fusion.4 = f32[128,2688]{1,0:T(8,128)S(1)} fusion(bf16[128,6144]{1,0:T(8,128)(2,1)} %all-gather.2.cloned.1.call-done, bf16[1,6144,2688]{2,1,0:T(8,128)(2,1)} %param.9), kind=kOutput, calls=%fused_computation.7 | convolution fusion | flops 4227858432 | bytes 35979264 | tf_op jit(solution)/shard_map/dot_general | solution.py:37
  62.3 0.0 copy-done.2
  62.3 25.0 %fusion.6 = bf16[128,6144]{1,0:T(8,128)(2,1)} fusion(bf16[1,2688,6144]{2,1,0:T(8,128)(2,1)} %param.11, bf16[128,6144]{1,0:T(8,128)(2,1)S(1)} %copy-done.2, bf16[1,6144,2688]{2,1,0:T(8,128)(2,1)} %param.10, f32[128,2688]{1,0:T(8,128)S(1)} %fusion.4), kind=kOutput, calls=%fused_computation.9 | convolution fusion | flops 8458567680 | bytes 70582272 | tf_op jit(solution)/shard_map/dot_general | solution.py:41
  87.3 0.0 copy-start.3
  87.3 0.0 reduce-scatter.2.cloned.1.call-update
  87.3 10.4 %reduce-scatter.2.cloned.1.call-done = bf16[64,6144]{1,0:T(8,128)(2,1)} async-done(((bf16[128,6144]{1,0:T(8,128)(2,1)}), bf16[64,6144]{1,0:T(8,128)(2,1)}) %reduce-scatter.2.cloned.1.call-update) | async-done | bytes 786448 | tf_op jit(solution)/shard_map/reduce_scatter | solution.py:40
  97.7 5.8 %all-to-all-start.1 = ((bf16[8,8,6144]{2,1,0:T(8,128)(2,1)}), bf16[8,8,6144]{2,1,0:T(8,128)(2,1)S(1)}, u32[]{:S(2)}, u32[]{:S(2)}) async-start(bf16[8,8,6144]{2,1,0:T(8,128)(2,1)} %bitcast.34), calls=%async_computation.2 | async-start | bytes 1572864 | tf_op jit(solution)/shard_map/all_to_all | solution.py:47
  103.5 0.1 reduce_sum.32
  103.6 0.0 copy-done.3
  103.6 0.1 copy.12
  103.7 20.4 %all-to-all-done.1 = bf16[8,8,6144]{2,1,0:T(8,128)(2,1)S(1)} async-done(((bf16[8,8,6144]{2,1,0:T(8,128)(2,1)}), bf16[8,8,6144]{2,1,0:T(8,128)(2,1)S(1)}, u32[]{:S(2)}, u32[]{:S(2)}) %all-to-all-start.1) | async-done | bytes 786464 | tf_op jit(solution)/shard_map/all_to_all | solution.py:47
  124.1 0.0 copy-start.1
  124.1 0.8 gather_fusion.1
  124.9 0.1 gather.12
  125.1 1.3 multiply_reduce_fusion
  126.3 0.0 copy-done.1
  (10 shorter events, 0.1 us)
Async XLA Ops:
  6.5 2.2 %copy-start = (bf16[8,6144]{1,0:T(8,128)(2,1)S(1)}, bf16[8,6144]{1,0:T(8,128)(2,1)}, u32[]{:S(2)}) copy-start(bf16[8,6144]{1,0:T(8,128)(2,1)} %param.6) | copy-start | bytes 294916
  6.5 39.7 %all-gather.2.cloned.1.call-start = ((), (), s32[]{:S(2)}) async-start(), calls=%async_computation.3 | async-start | bytes 2359296 | tf_op jit(solution)/shard_map/all_gather | solution.py:36
  37.3 60.5 %reduce-scatter.2.cloned.1.call-start = ((), (), s32[]{:S(2)}) async-start(), calls=%async_computation.4 | async-start | bytes 2359296 | tf_op jit(solution)/shard_map/reduce_scatter | solution.py:40
  46.2 16.1 %copy-start.2 = (bf16[128,6144]{1,0:T(8,128)(2,1)S(1)}, bf16[128,6144]{1,0:T(8,128)(2,1)}, u32[]{:S(2)}) copy-start(bf16[128,6144]{1,0:T(8,128)(2,1)} %all-gather.2.cloned.1.call-done) | copy-start | bytes 4718596
  87.3 16.3 %copy-start.3 = (s32[8,4]{0,1:T(4,128)S(1)}, s32[8,4]{0,1:T(4,128)}, u32[]{:S(2)}) copy-start(s32[8,4]{0,1:T(4,128)} %param.8) | copy-start | bytes 388
  97.7 26.4 %all-to-all-start.1 = ((bf16[8,8,6144]{2,1,0:T(8,128)(2,1)}), bf16[8,8,6144]{2,1,0:T(8,128)(2,1)S(1)}, u32[]{:S(2)}, u32[]{:S(2)}) async-start(bf16[8,8,6144]{2,1,0:T(8,128)(2,1)} %bitcast.34), calls=%async_computation.2 | async-start | bytes 1572864 | tf_op jit(solution)/shard_map/all_to_all | solution.py:47
  124.1 2.2 %copy-start.1 = (bf16[8,6144]{1,0:T(8,128)(2,1)S(1)}, bf16[8,6144]{1,0:T(8,128)(2,1)}, u32[]{:S(2)}) copy-start(bf16[8,6144]{1,0:T(8,128)(2,1)} %param.6) | copy-start | bytes 294916
Sparse Core Ops, SparseCore 0:
  37.4 8.8 all-gather.1
  87.5 10.2 reduce-scatter.1
where the time goes:
time: 133 us
  matrix products  41 us (31%)
  waiting for transfers between devices  39.7 us (30%)
  blocking collectives  27.3 us (21%)
  between operations  13.5 us (10%)
  starting transfers between devices  5.84 us (4%)
  local copies, waits for them, and re-layouts  3.92 us (3%)
  other arithmetic  1.81 us (1%)
    all_to_all x1, blocking collectives, shards(): lax.all_to_all(outgoing, 'expert', split_axis=0, concat_axis=0, tiled=True)  27.3 us
    dot_general x1, matrix products, shards(): jnp.dot(hidden, down_mat, preferred_element_type=jnp.float32)  25 us
    all_to_all x1, waiting for transfers between devices, shards(): lax.all_to_all(expert_rows, 'expert', split_axis=0, concat_axis=0, tiled=...  20.4 us
    dot_general x1, matrix products, shards(): gate_val = jnp.dot(row_piece, gate_mat, preferred_element_type=jnp.float32)  16.1 us
    reduce_scatter x1, waiting for transfers between devices, shards(): lax.psum_scatter(jnp.dot(hidden, down_mat, preferred_element_type=jnp.flo...  10.4 us
    all_gather x1, waiting for transfers between devices, shards(): lax.all_gather(arrived.reshape(-1, model_width), 'tensor', axis=0, tiled=...  8.95 us
    all_to_all x1, starting transfers between devices, shards(): lax.all_to_all(expert_rows, 'expert', split_axis=0, concat_axis=0, tiled=...  5.8 us
  transfers between devices with their start and end apart: 3, of which 3 were waited for; matrix products, arithmetic and copies ran while one was open for 0% of the time, Pallas kernels for 0%

commit v1 on v0

--- a/solution.py
+++ b/solution.py
@@ -1,9 +1,284 @@
+import functools
+
 import jax
 import jax.numpy as jnp
 from jax import lax
+from jax.experimental import pallas as pl
+from jax.experimental.pallas import tpu as pltpu
 from jax.sharding import PartitionSpec as P
 
 CAP = 8
+LANES = 128
+K_SLOTS = 3
+D_SLOTS = 6
+MESH = pl.DeviceIdType.MESH
+
+
+def divisor(n, most, unit):
+    best = unit
+    for d in range(unit, most + 1, unit):
+        if n % d == 0:
+            best = d
+    return best
+
+
+def pieces(n, width):
+    return [(c, min(width, n - c)) for c in range(0, n, width)]
+
+
+def fused_kernel(
+    Z, X, T, KB, NB,
+    tok_ref, routes_ref, gate_ref, wg_hbm, wu_hbm, wd_hbm, out_ref,
+    xraw, xb, coef, wg, wu, wd, acc_g, acc_u, hid,
+    part, got_a, send_b, own_b, got_b, send_c, got_c,
+    wg_sem, wu_sem, wd_sem, xs_sem, xr_sem,
+    as_sem, ar_sem, bs_sem, br_sem, cs_sem, cr_sem,
+):
+    E = Z * X
+    R, D = tok_ref.shape
+    F = wg_hbm.shape[2]
+    ROWS = E * T * R
+    KN = D // KB
+    ND = D // NB
+    e = lax.axis_index("expert")
+    t = lax.axis_index("tensor")
+    x = lax.rem(e, X)
+    z = e // X
+    xo = 1 - x
+    to = 1 - t
+
+    def gate_copies(k, slot):
+        rows = pl.ds(pl.multiple_of(k * KB, KB), KB)
+        return (
+            pltpu.make_async_copy(wg_hbm.at[0, rows, :], wg.at[slot], wg_sem.at[slot]),
+            pltpu.make_async_copy(wu_hbm.at[0, rows, :], wu.at[slot], wu_sem.at[slot]),
+        )
+
+    def down_copy(i, slot):
+        cols = pl.ds(pl.multiple_of(i * NB, NB), NB)
+        return pltpu.make_async_copy(wd_hbm.at[0, :, cols], wd.at[slot], wd_sem.at[slot])
+
+    for k in range(K_SLOTS):
+        for c in gate_copies(k, k):
+            c.start()
+    for i in range(D_SLOTS):
+        down_copy(i, i).start()
+
+    def block(tt, xx, zz):
+        return tt * E + xx * Z + zz
+
+    mine = block(t, x, z)
+    zs = [lax.rem(z + d, Z) for d in range(Z)]
+    at_z = [{"expert": zz * X + x, "tensor": t} for zz in zs]
+    at_x = {"expert": z * X + xo, "tensor": t}
+    at_t = {"expert": e, "tensor": to}
+    peers = at_z[1:] + [at_x, at_t]
+
+    barrier = pltpu.get_barrier_semaphore()
+    for p in peers:
+        pl.semaphore_signal(barrier, inc=1, device_id=p, device_id_type=MESH)
+
+    fixed = gate_ref[...].astype(jnp.float32)
+    mix = fixed / jnp.sum(fixed, axis=1, keepdims=True)
+    routes = routes_ref[...]
+    lane = lax.broadcasted_iota(jnp.int32, (R, LANES), 1)
+    expert_of = lax.rem(lane, E)
+    c = jnp.zeros((R, LANES), jnp.float32)
+    for k in range(routes.shape[1]):
+        c = c + jnp.where(expert_of == routes[:, k:k + 1], mix[:, k:k + 1], 0.0)
+    hi = c.astype(jnp.bfloat16).astype(jnp.float32)
+    mid = (c - hi).astype(jnp.bfloat16).astype(jnp.float32)
+    low = c - hi - mid
+    term = lane // E
+    c = jnp.where(term == 0, hi, jnp.where(term == 1, mid, jnp.where(term == 2, low, 0.0)))
+    xraw[mine, :, :D] = tok_ref[...]
+    xraw[mine, :, D:] = c.astype(jnp.bfloat16)
+
+    pl.semaphore_wait(barrier, len(peers))
+
+    sent = []
+
+    def send(b, where):
+        n = len(sent)
+        cp = pltpu.make_async_remote_copy(
+            src_ref=xraw.at[b], dst_ref=xraw.at[b], send_sem=xs_sem.at[n], recv_sem=xr_sem.at[b],
+            device_id=where, device_id_type=MESH)
+        cp.start()
+        sent.append(cp)
+
+    def arrived(b):
+        pltpu.make_async_remote_copy(
+            src_ref=xraw.at[b], dst_ref=xraw.at[b], send_sem=xs_sem.at[0], recv_sem=xr_sem.at[b],
+            device_id=at_t, device_id_type=MESH).wait_recv()
+
+    send(mine, at_x)
+    for d in range(1, Z):
+        send(mine, at_z[d])
+    send(mine, at_t)
+    for d in range(1, Z):
+        b = block(t, x, zs[d])
+        arrived(b)
+        send(b, at_x)
+        send(b, at_t)
+    for d in range(Z):
+        b = block(t, xo, zs[d])
+        arrived(b)
+        send(b, at_t)
+    for d in range(Z):
+        arrived(block(to, x, zs[d]))
+    for d in range(Z):
+        arrived(block(to, xo, zs[d]))
+
+    @pl.loop(0, E * T // 2)
+    def _(p):
+        rows = pl.ds(pl.multiple_of(p * 2 * R, 2 * R), 2 * R)
+        for c0, w in pieces(D, 1024):
+            two = xraw[pl.ds(p * 2, 2), :, c0:c0 + w].astype(jnp.float32)
+            xb[rows, c0:c0 + w] = two.reshape(2 * R, w).astype(jnp.bfloat16)
+        two = xraw[pl.ds(p * 2, 2), :, D:].astype(jnp.float32).reshape(2 * R, LANES)
+        at = lax.broadcasted_iota(jnp.int32, (2 * R, LANES), 1)
+        own = jnp.where((lax.rem(at, E) == e) & (at < 3 * E), two, 0.0)
+        coef[rows, :] = jnp.broadcast_to(jnp.sum(own, axis=1, keepdims=True), (2 * R, LANES))
+
+    for c0, w in pieces(F, 512):
+        acc_g[:, c0:c0 + w] = jnp.zeros((ROWS, w), jnp.float32)
+        acc_u[:, c0:c0 + w] = jnp.zeros((ROWS, w), jnp.float32)
+
+    @pl.loop(0, KN)
+    def _(k):
+        slot = lax.rem(k, K_SLOTS)
+        xk = xb[:, pl.ds(pl.multiple_of(k * KB, KB), KB)]
+        for cp, w_ref, acc in zip(gate_copies(k, slot), (wg, wu), (acc_g, acc_u)):
+            cp.wait()
+            for c0, w in pieces(F, 512):
+                acc[:, c0:c0 + w] += jnp.dot(
+                    xk, w_ref[slot, :, c0:c0 + w], preferred_element_type=jnp.float32)
+
+        @pl.when(k + K_SLOTS < KN)
+        def _():
+            for cp in gate_copies(k + K_SLOTS, slot):
+                cp.start()
+
+    for c0, w in pieces(F, 512):
+        g = acc_g[:, c0:c0 + w]
+        hid[:, c0:c0 + w] = (g / (1.0 + jnp.exp(-g)) * acc_u[:, c0:c0 + w]).astype(jnp.bfloat16)
+
+    def copy_a(i):
+        return pltpu.make_async_remote_copy(
+            src_ref=part.at[i, to], dst_ref=got_a.at[i], send_sem=as_sem.at[i], recv_sem=ar_sem.at[i],
+            device_id=at_t, device_id_type=MESH)
+
+    def copy_b(i):
+        return pltpu.make_async_remote_copy(
+            src_ref=send_b.at[i], dst_ref=got_b.at[i], send_sem=bs_sem.at[i], recv_sem=br_sem.at[i],
+            device_id=at_x, device_id_type=MESH)
+
+    def copy_c(i, d):
+        return pltpu.make_async_remote_copy(
+            src_ref=send_c.at[i, zs[d]], dst_ref=got_c.at[i, d - 1],
+            send_sem=cs_sem.at[i, d - 1], recv_sem=cr_sem.at[i, d - 1],
+            device_id=at_z[d], device_id_type=MESH)
+
+    LAG_A, LAG_B, LAG_C = 1, 3, 5
+
+    @pl.loop(0, ND + LAG_C)
+    def _(i):
+        @pl.when(i < ND)
+        def _():
+            slot = lax.rem(i, D_SLOTS)
+            down_copy(i, slot).wait()
+            y = jnp.dot(hid[...], wd[slot], preferred_element_type=jnp.float32) * coef[:, 0:1]
+            part[i] = y.reshape(T, E, R, NB).astype(jnp.bfloat16)
+            copy_a(i).start()
+
+            @pl.when(i + D_SLOTS < ND)
+            def _():
+                down_copy(i + D_SLOTS, slot).start()
+
+        @pl.when((i >= LAG_A) & (i < ND + LAG_A))
+        def _():
+            j = i - LAG_A
+            copy_a(j).wait_recv()
+            theirs = pl.ds(xo * Z, Z)
+            ours = pl.ds(x * Z, Z)
+            send_b[j] = (part[j, t, theirs].astype(jnp.float32)
+                         + got_a[j, theirs].astype(jnp.float32)).astype(jnp.bfloat16)
+            copy_b(j).start()
+            own_b[j] = part[j, t, ours].astype(jnp.float32) + got_a[j, ours].astype(jnp.float32)
+
+        @pl.when((i >= LAG_B) & (i < ND + LAG_B))
+        def _():
+            j = i - LAG_B
+            copy_b(j).wait_recv()
+            send_c[j] = (own_b[j] + got_b[j].astype(jnp.float32)).astype(jnp.bfloat16)
+            for d in range(1, Z):
+                copy_c(j, d).start()
+
+        @pl.when(i >= LAG_C)
+        def _():
+            j = i - LAG_C
+            total = send_c[j, z].astype(jnp.float32)
+            for d in range(1, Z):
+                copy_c(j, d).wait_recv()
+                total = total + got_c[j, d - 1].astype(jnp.float32)
+            out_ref[:, pl.ds(pl.multiple_of(j * NB, NB), NB)] = total.astype(jnp.bfloat16)
+
+    for cp in sent:
+        cp.wait_send()
+
+    @pl.loop(0, ND)
+    def _(i):
+        copy_a(i).wait_send()
+        copy_b(i).wait_send()
+        for d in range(1, Z):
+            copy_c(i, d).wait_send()
+
+
+def fused_shards(tokens, routes, gate_fixed, w_gate, w_up, w_down):
+    E, T = lax.axis_size("expert"), lax.axis_size("tensor")
+    X = 2
+    Z = E // X
+    R, D = tokens.shape
+    F = w_gate.shape[2]
+    KB = divisor(D, 768, 256)
+    NB = divisor(D, 512, 256)
+    ND = D // NB
+    rows = E * T * R
+    bf, f32 = jnp.bfloat16, jnp.float32
+    vm = pltpu.VMEM
+    dma = pltpu.SemaphoreType.DMA
+    vmem, any_ = pl.BlockSpec(memory_space=vm), pl.BlockSpec(memory_space=pl.ANY)
+    return pl.pallas_call(
+        functools.partial(fused_kernel, Z, X, T, KB, NB),
+        out_shape=jax.ShapeDtypeStruct((R, D), bf),
+        in_specs=[vmem, vmem, vmem, any_, any_, any_],
+        out_specs=vmem,
+        scratch_shapes=[
+            vm((E * T, R, D + LANES), bf),
+            vm((rows, D), bf),
+            vm((rows, LANES), f32),
+            vm((K_SLOTS, KB, F), bf),
+            vm((K_SLOTS, KB, F), bf),
+            vm((D_SLOTS, F, NB), bf),
+            vm((rows, F), f32),
+            vm((rows, F), f32),
+            vm((rows, F), bf),
+            vm((ND, T, E, R, NB), bf),
+            vm((ND, E, R, NB), bf),
+            vm((ND, Z, R, NB), bf),
+            vm((ND, Z, R, NB), f32),
+            vm((ND, Z, R, NB), bf),
+            vm((ND, Z, R, NB), bf),
+            vm((ND, Z - 1, R, NB), bf),
+            dma((K_SLOTS,)), dma((K_SLOTS,)), dma((D_SLOTS,)),
+            dma((E * T - 1,)), dma((E * T,)),
+            dma((ND,)), dma((ND,)), dma((ND,)), dma((ND,)), dma((ND, Z - 1)), dma((ND, Z - 1)),
+        ],
+        compiler_params=pltpu.CompilerParams(
+            collective_id=0, has_side_effects=True, vmem_limit_bytes=60 * 1024 * 1024),
+        cost_estimate=pl.CostEstimate(
+            flops=6 * rows * D * F, bytes_accessed=6 * D * F, transcendentals=rows * F),
+    )(tokens, routes, gate_fixed, w_gate, w_up, w_down)
 
 
 def slot_table(route_block, n_experts):
@@ -62,8 +337,9 @@
         P("expert", None, "tensor"),
         P("expert", "tensor", None),
     )
+    fits = (mesh.shape["tensor"] == 2 and mesh.shape["expert"] % 4 == 0)
     return jax.shard_map(
-        shards,
+        fused_shards if fits else shards,
         mesh=mesh,
         in_specs=placed,
         out_specs=P(("group", "expert", "tensor"), None),

time: 133 us -> 69.8 us (0.52)
  Pallas kernels: 0 us -> 65.3 us
  matrix products: 41 us -> 0 us
  waiting for transfers between devices: 39.7 us -> 0 us
  blocking collectives: 27.3 us -> 0 us
  between operations: 13.5 us -> 0.01 us
  starting transfers between devices: 5.84 us -> 0 us
  other arithmetic: 1.81 us -> 0 us
    pallas_call x0 -> x1, Pallas kernels: none -> 65.3 us  [fused_shards(): pl.pallas_call(functools.partial(fused_kernel, Z, X, T, KB, NB), out_shap...]
    dot_general x2 -> x0, matrix products: 41 us -> none  [the longest x1 25 us: shards(): jnp.dot(hidden, down_mat, preferred_element_type=jnp.float32)]
    all_to_all x1 -> x0, blocking collectives: 27.3 us -> none  [shards(): lax.all_to_all(outgoing, 'expert', split_axis=0, concat_axis=0, tiled=True)]
    all_to_all x1 -> x0, waiting for transfers between devices: 20.4 us -> none  [shards(): lax.all_to_all(expert_rows, 'expert', split_axis=0, concat_axis=0, tiled=...]
    reduce_scatter x1 -> x0, waiting for transfers between devices: 10.4 us -> none  [shards(): lax.psum_scatter(jnp.dot(hidden, down_mat, preferred_element_type=jnp.flo...]
    all_gather x1 -> x0, waiting for transfers between devices: 8.95 us -> none  [shards(): lax.all_gather(arrived.reshape(-1, model_width), 'tensor', axis=0, tiled=...]
    all_to_all x1 -> x0, starting transfers between devices: 5.8 us -> none  [shards(): lax.all_to_all(expert_rows, 'expert', split_axis=0, concat_axis=0, tiled=...]
    unnamed x9 -> x3, local copies, waits for them, and re-layouts: 0.8 us -> 4.24 us
  transfers between devices with their start and end apart: 3 -> 0, of which waited for: 3 -> 0; matrix products, arithmetic and copies ran while one was open for 0% -> 0% of each run, Pallas kernels for 0% -> 0%
where the time goes in v1:
time: 69.8 us; the launch traced here: 69.6 us
  Pallas kernels  65.3 us (94%)
  local copies, waits for them, and re-layouts  4.24 us (6%)
    pallas_call x1, Pallas kernels, fused_shards(): pl.pallas_call(functools.partial(fused_kernel, Z, X, T, KB, NB), out_shap...  65.3 us
    unnamed x3, local copies, waits for them, and re-layouts  4.24 us

profile of v1, /device:TPU:0, one launch (start us, length us, event | category | flops | bytes accessed | tf_op | source)
XLA Modules:
  0.0 69.6 jit_solution(12086778601786473717)
XLA Ops:
  0.0 1.3 %copy.7.routes_ref = s32[8,4]{1,0:T(8,128)} copy(s32[8,4]{0,1:T(4,128)} %param.7) | data formatting | bytes 256 | tf_op args[1]
  1.3 1.3 %copy.8.gate_ref = s32[8,4]{1,0:T(8,128)} copy(s32[8,4]{0,1:T(4,128)} %param.8) | data formatting | bytes 256 | tf_op args[2]
  2.7 65.3 %shard_map.64 = bf16[8,6144]{1,0:T(8,128)(2,1)} custom-call(bf16[8,6144]{1,0:T(8,128)(2,1)} %tok_ref.1, s32[8,4]{1,0:T(8,128)} %copy.7.routes_ref, s32[8,4]{1,0:T(8,128)} %copy.8.gate_ref, bf16[1,6144,2688]{2,1,0:T(8,128)(2,1)} %wg_hbm.1, bf16[1,6144,2688]{2,1,0:T(8,128)(2,1)} %wu_hbm.1, bf16[1,2688,6144]{2,1,0:T(8,128)(2,1)} %wd_hbm.1), custom_call_target="tpu_custom_call" | custom-call | flops 12683575296 | bytes 99090432 | tf_op jit(solution)/shard_map/pallas_call | solution.py:251
  68.0 1.5 %copy.10 = bf16[8,6144]{1,0:T(8,128)(2,1)} copy(bf16[8,6144]{1,0:T(8,128)(2,1)} %shard_map.64) | data formatting | bytes 196608

commit v2 on v1

--- a/solution.py
+++ b/solution.py
@@ -9,8 +9,9 @@
 
 CAP = 8
 LANES = 128
-K_SLOTS = 3
-D_SLOTS = 6
+K_SLOTS = 4
+D_SLOTS = 4
+STEPS = 2
 MESH = pl.DeviceIdType.MESH
 
 
@@ -40,6 +41,8 @@
     ROWS = E * T * R
     KN = D // KB
     ND = D // NB
+    CW = STEPS * KB
+    CN = D // CW
     e = lax.axis_index("expert")
     t = lax.axis_index("tensor")
     x = lax.rem(e, X)
@@ -61,8 +64,6 @@
     for k in range(K_SLOTS):
         for c in gate_copies(k, k):
             c.start()
-    for i in range(D_SLOTS):
-        down_copy(i, i).start()
 
     def block(tt, xx, zz):
         return tt * E + xx * Z + zz
@@ -91,73 +92,102 @@
     low = c - hi - mid
     term = lane // E
     c = jnp.where(term == 0, hi, jnp.where(term == 1, mid, jnp.where(term == 2, low, 0.0)))
-    xraw[mine, :, :D] = tok_ref[...]
-    xraw[mine, :, D:] = c.astype(jnp.bfloat16)
+    for n in range(CN):
+        xraw[n, mine, :, :CW] = tok_ref[:, n * CW:(n + 1) * CW]
+        xraw[n, mine, :, CW:] = c.astype(jnp.bfloat16)
 
     pl.semaphore_wait(barrier, len(peers))
 
-    sent = []
-
-    def send(b, where):
-        n = len(sent)
-        cp = pltpu.make_async_remote_copy(
-            src_ref=xraw.at[b], dst_ref=xraw.at[b], send_sem=xs_sem.at[n], recv_sem=xr_sem.at[b],
+    from_own = [(mine, at_z[1]), (mine, at_x)] + [(mine, at_z[d]) for d in range(2, Z)] + [(mine, at_t)]
+    from_z = [(block(t, x, zs[d]), w) for d in range(1, Z) for w in (at_x, at_t)]
+    from_x = [(block(t, xo, zs[d]), at_t) for d in range(Z)]
+    from_t = [block(to, xx, zs[d]) for xx in (x, xo) for d in range(Z)]
+    routes_out = from_own + from_z + from_x
+
+    def token_copy(n, k):
+        b, where = routes_out[k]
+        return pltpu.make_async_remote_copy(
+            src_ref=xraw.at[n, b], dst_ref=xraw.at[n, b], send_sem=xs_sem.at[n, k], recv_sem=xr_sem.at[n, b],
             device_id=where, device_id_type=MESH)
-        cp.start()
-        sent.append(cp)
-
-    def arrived(b):
+
+    def arrived(n, b):
         pltpu.make_async_remote_copy(
-            src_ref=xraw.at[b], dst_ref=xraw.at[b], send_sem=xs_sem.at[0], recv_sem=xr_sem.at[b],
+            src_ref=xraw.at[n, b], dst_ref=xraw.at[n, b], send_sem=xs_sem.at[n, 0], recv_sem=xr_sem.at[n, b],
             device_id=at_t, device_id_type=MESH).wait_recv()
 
-    send(mine, at_x)
-    for d in range(1, Z):
-        send(mine, at_z[d])
-    send(mine, at_t)
-    for d in range(1, Z):
-        b = block(t, x, zs[d])
-        arrived(b)
-        send(b, at_x)
-        send(b, at_t)
-    for d in range(Z):
-        b = block(t, xo, zs[d])
-        arrived(b)
-        send(b, at_t)
-    for d in range(Z):
-        arrived(block(to, x, zs[d]))
-    for d in range(Z):
-        arrived(block(to, xo, zs[d]))
+    def pass_z(n):
+        k = len(from_own)
+        for d in range(1, Z):
+            arrived(n, block(t, x, zs[d]))
+            token_copy(n, k).start()
+            token_copy(n, k + 1).start()
+            k += 2
+
+    def pass_x(n):
+        k = len(from_own) + len(from_z)
+        for d in range(Z):
+            arrived(n, block(t, xo, zs[d]))
+            token_copy(n, k).start()
+            k += 1
+
+    for n in range(CN):
+        for k in range(len(from_own)):
+            token_copy(n, k).start()
+    for c0, w in pieces(F, 512):
+        acc_g[:, c0:c0 + w] = jnp.zeros((ROWS, w), jnp.float32)
+        acc_u[:, c0:c0 + w] = jnp.zeros((ROWS, w), jnp.float32)
+    pass_z(0)
+    if CN > 1:
+        pass_z(1)
+    pass_x(0)
+
+    @pl.loop(0, CN)
+    def _(n):
+        for b in from_t:
+            arrived(n, b)
+
+        @pl.loop(0, E * T // 2)
+        def _(p):
+            rows = pl.ds(pl.multiple_of(p * 2 * R, 2 * R), 2 * R)
+            for j in range(STEPS):
+                two = xraw[n, pl.ds(p * 2, 2), :, j * KB:(j + 1) * KB].astype(jnp.float32)
+                xb[j, rows, :] = two.reshape(2 * R, KB).astype(jnp.bfloat16)
+
+        for j in range(STEPS):
+            k = n * STEPS + j
+            slot = lax.rem(k, K_SLOTS)
+            for cp, w_ref, acc in zip(gate_copies(k, slot), (wg, wu), (acc_g, acc_u)):
+                cp.wait()
+                for c0, w in pieces(F, 512):
+                    acc[:, c0:c0 + w] += jnp.dot(
+                        xb[j], w_ref[slot, :, c0:c0 + w], preferred_element_type=jnp.float32)
+
+            @pl.when(k + K_SLOTS < KN)
+            def _():
+                for cp in gate_copies(k + K_SLOTS, slot):
+                    cp.start()
+
+            @pl.when(k + K_SLOTS == KN - 1)
+            def _():
+                for i in range(D_SLOTS):
+                    down_copy(i, i).start()
+
+            if j == 0:
+                @pl.when(n + 1 < CN)
+                def _():
+                    pass_x(n + 1)
+
+                @pl.when(n + 2 < CN)
+                def _():
+                    pass_z(n + 2)
 
     @pl.loop(0, E * T // 2)
     def _(p):
         rows = pl.ds(pl.multiple_of(p * 2 * R, 2 * R), 2 * R)
-        for c0, w in pieces(D, 1024):
-            two = xraw[pl.ds(p * 2, 2), :, c0:c0 + w].astype(jnp.float32)
-            xb[rows, c0:c0 + w] = two.reshape(2 * R, w).astype(jnp.bfloat16)
-        two = xraw[pl.ds(p * 2, 2), :, D:].astype(jnp.float32).reshape(2 * R, LANES)
+        two = xraw[0, pl.ds(p * 2, 2), :, CW:].astype(jnp.float32).reshape(2 * R, LANES)
         at = lax.broadcasted_iota(jnp.int32, (2 * R, LANES), 1)
         own = jnp.where((lax.rem(at, E) == e) & (at < 3 * E), two, 0.0)
         coef[rows, :] = jnp.broadcast_to(jnp.sum(own, axis=1, keepdims=True), (2 * R, LANES))
-
-    for c0, w in pieces(F, 512):
-        acc_g[:, c0:c0 + w] = jnp.zeros((ROWS, w), jnp.float32)
-        acc_u[:, c0:c0 + w] = jnp.zeros((ROWS, w), jnp.float32)
-
-    @pl.loop(0, KN)
-    def _(k):
-        slot = lax.rem(k, K_SLOTS)
-        xk = xb[:, pl.ds(pl.multiple_of(k * KB, KB), KB)]
-        for cp, w_ref, acc in zip(gate_copies(k, slot), (wg, wu), (acc_g, acc_u)):
-            cp.wait()
-            for c0, w in pieces(F, 512):
-                acc[:, c0:c0 + w] += jnp.dot(
-                    xk, w_ref[slot, :, c0:c0 + w], preferred_element_type=jnp.float32)
-
-        @pl.when(k + K_SLOTS < KN)
-        def _():
-            for cp in gate_copies(k + K_SLOTS, slot):
-                cp.start()
 
     for c0, w in pieces(F, 512):
         g = acc_g[:, c0:c0 + w]
@@ -179,7 +209,7 @@
             send_sem=cs_sem.at[i, d - 1], recv_sem=cr_sem.at[i, d - 1],
             device_id=at_z[d], device_id_type=MESH)
 
-    LAG_A, LAG_B, LAG_C = 1, 3, 5
+    LAG_A, LAG_B, LAG_C = 2, 5, 8
 
     @pl.loop(0, ND + LAG_C)
     def _(i):
@@ -223,8 +253,10 @@
                 total = total + got_c[j, d - 1].astype(jnp.float32)
             out_ref[:, pl.ds(pl.multiple_of(j * NB, NB), NB)] = total.astype(jnp.bfloat16)
 
-    for cp in sent:
-        cp.wait_send()
+    @pl.loop(0, CN)
+    def _(n):
+        for k in range(len(routes_out)):
+            token_copy(n, k).wait_send()
 
     @pl.loop(0, ND)
     def _(i):
@@ -243,6 +275,8 @@
     KB = divisor(D, 768, 256)
     NB = divisor(D, 512, 256)
     ND = D // NB
+    CW = STEPS * KB
+    CN = D // CW
     rows = E * T * R
     bf, f32 = jnp.bfloat16, jnp.float32
     vm = pltpu.VMEM
@@ -254,8 +288,8 @@
         in_specs=[vmem, vmem, vmem, any_, any_, any_],
         out_specs=vmem,
         scratch_shapes=[
-            vm((E * T, R, D + LANES), bf),
-            vm((rows, D), bf),
+            vm((CN, E * T, R, CW + LANES), bf),
+            vm((STEPS, rows, KB), bf),
             vm((rows, LANES), f32),
             vm((K_SLOTS, KB, F), bf),
             vm((K_SLOTS, KB, F), bf),
@@ -271,11 +305,11 @@
             vm((ND, Z, R, NB), bf),
             vm((ND, Z - 1, R, NB), bf),
             dma((K_SLOTS,)), dma((K_SLOTS,)), dma((D_SLOTS,)),
-            dma((E * T - 1,)), dma((E * T,)),
+            dma((CN, E * T - 1)), dma((CN, E * T)),
             dma((ND,)), dma((ND,)), dma((ND,)), dma((ND,)), dma((ND, Z - 1)), dma((ND, Z - 1)),
         ],
         compiler_params=pltpu.CompilerParams(
-            collective_id=0, has_side_effects=True, vmem_limit_bytes=60 * 1024 * 1024),
+            collective_id=0, has_side_effects=True, vmem_limit_bytes=61 * 1024 * 1024),
         cost_estimate=pl.CostEstimate(
             flops=6 * rows * D * F, bytes_accessed=6 * D * F, transcendentals=rows * F),
     )(tokens, routes, gate_fixed, w_gate, w_up, w_down)

time: 69.8 us -> 59.9 us (0.86)
  Pallas kernels: 65.3 us -> 55.5 us
    pallas_call x1, Pallas kernels: 65.3 us -> 55.5 us  [fused_shards(): pl.pallas_call(functools.partial(fused_kernel, Z, X, T, KB, NB), out_shap...]
where the time goes in v2:
time: 59.9 us; the launch traced here: 59.7 us
  Pallas kernels  55.5 us (93%)
  local copies, waits for them, and re-layouts  4.24 us (7%)
    pallas_call x1, Pallas kernels, fused_shards(): pl.pallas_call(functools.partial(fused_kernel, Z, X, T, KB, NB), out_shap...  55.5 us
    unnamed x3, local copies, waits for them, and re-layouts  4.24 us

profile of v2, /device:TPU:0, one launch (start us, length us, event | category | flops | bytes accessed | tf_op | source)
XLA Modules:
  0.0 59.7 jit_solution(9218258707421285844)
XLA Ops:
  0.0 1.3 %copy.7.routes_ref = s32[8,4]{1,0:T(8,128)} copy(s32[8,4]{0,1:T(4,128)} %param.7) | data formatting | bytes 256 | tf_op args[1]
  1.3 1.3 %copy.8.gate_ref = s32[8,4]{1,0:T(8,128)} copy(s32[8,4]{0,1:T(4,128)} %param.8) | data formatting | bytes 256 | tf_op args[2]
  2.7 55.5 %shard_map.64 = bf16[8,6144]{1,0:T(8,128)(2,1)} custom-call(bf16[8,6144]{1,0:T(8,128)(2,1)} %tok_ref.1, s32[8,4]{1,0:T(8,128)} %copy.7.routes_ref, s32[8,4]{1,0:T(8,128)} %copy.8.gate_ref, bf16[1,6144,2688]{2,1,0:T(8,128)(2,1)} %wg_hbm.1, bf16[1,6144,2688]{2,1,0:T(8,128)(2,1)} %wu_hbm.1, bf16[1,2688,6144]{2,1,0:T(8,128)(2,1)} %wd_hbm.1), custom_call_target="tpu_custom_call" | custom-call | flops 12683575296 | bytes 99090432 | tf_op jit(solution)/shard_map/pallas_call | solution.py:285
  58.2 1.5 %copy.10 = bf16[8,6144]{1,0:T(8,128)(2,1)} copy(bf16[8,6144]{1,0:T(8,128)(2,1)} %shard_map.64) | data formatting | bytes 196608

commit v3 on v2

--- a/solution.py
+++ b/solution.py
@@ -10,7 +10,7 @@
 CAP = 8
 LANES = 128
 K_SLOTS = 4
-D_SLOTS = 4
+D_SLOTS = 3
 STEPS = 2
 MESH = pl.DeviceIdType.MESH
 
@@ -273,7 +273,7 @@
     R, D = tokens.shape
     F = w_gate.shape[2]
     KB = divisor(D, 768, 256)
-    NB = divisor(D, 512, 256)
+    NB = divisor(D, 768, 256)
     ND = D // NB
     CW = STEPS * KB
     CN = D // CW

time: 59.9 us -> 58.1 us (0.970)
  Pallas kernels: 55.5 us -> 53.6 us
    pallas_call x1, Pallas kernels: 55.5 us -> 53.6 us  [fused_shards(): pl.pallas_call(functools.partial(fused_kernel, Z, X, T, KB, NB), out_shap...]
where the time goes in v3:
time: 58.1 us; the launch traced here: 57.8 us
  Pallas kernels  53.6 us (92%)
  local copies, waits for them, and re-layouts  4.24 us (7%)
    pallas_call x1, Pallas kernels, fused_shards(): pl.pallas_call(functools.partial(fused_kernel, Z, X, T, KB, NB), out_shap...  53.6 us
    unnamed x3, local copies, waits for them, and re-layouts  4.24 us

profile of v3, /device:TPU:0, one launch (start us, length us, event | category | flops | bytes accessed | tf_op | source)
XLA Modules:
  0.0 57.8 jit_solution(12540235953470638747)
XLA Ops:
  0.0 1.3 %copy.7.routes_ref = s32[8,4]{1,0:T(8,128)} copy(s32[8,4]{0,1:T(4,128)} %param.7) | data formatting | bytes 256 | tf_op args[1]
  1.3 1.3 %copy.8.gate_ref = s32[8,4]{1,0:T(8,128)} copy(s32[8,4]{0,1:T(4,128)} %param.8) | data formatting | bytes 256 | tf_op args[2]
  2.7 53.6 %shard_map.64 = bf16[8,6144]{1,0:T(8,128)(2,1)} custom-call(bf16[8,6144]{1,0:T(8,128)(2,1)} %tok_ref.1, s32[8,4]{1,0:T(8,128)} %copy.7.routes_ref, s32[8,4]{1,0:T(8,128)} %copy.8.gate_ref, bf16[1,6144,2688]{2,1,0:T(8,128)(2,1)} %wg_hbm.1, bf16[1,6144,2688]{2,1,0:T(8,128)(2,1)} %wu_hbm.1, bf16[1,2688,6144]{2,1,0:T(8,128)(2,1)} %wd_hbm.1), custom_call_target="tpu_custom_call" | custom-call | flops 12683575296 | bytes 99090432 | tf_op jit(solution)/shard_map/pallas_call | solution.py:285
  56.3 1.5 %copy.10 = bf16[8,6144]{1,0:T(8,128)(2,1)} copy(bf16[8,6144]{1,0:T(8,128)(2,1)} %shard_map.64) | data formatting | bytes 196608
